TPU v7x, 32 devices: a whole 2x2x4 slice. The times are simulated.
32 devices in a mesh: ta: 4 (over z), gz: 4 (over y, core), gy: 2 (over x).
Axes of the slice: x: 2, y: 2, z: 4, core: 2. Of those that a mesh axis runs over, the one named last changes fastest.
Arguments:
- source: float32 [2, 4, 3, 16, 16, 256], P(None, None, None, 'ta', 'gz', 'gy'), may hold values from -6 to 6
- gauge_links: float32 [4, 2, 3, 3, 16, 16, 256], P(None, None, None, None, 'ta', 'gz', 'gy'), may hold values from -1 to 1, as said below
- near_null: bfloat16 [24, 2, 4, 3, 16, 16, 256], P(None, None, None, None, 'ta', 'gz', 'gy'), may hold values from -0.109375 to 0.109375
- w_first: float32 [9, 2, 1, 2, 4, 4], replicated, may hold values from -0.75 to 0.75
- w_second: float32 [9, 1, 2, 2, 4, 4], replicated, may hold values from -0.5 to 0.5
Outputs:
- network_out: float32 [2, 4, 3, 16, 16, 256], P(None, None, None, 'ta', 'gz', 'gy')
- coarse: float32 [2, 24, 4, 4, 16], P(None, None, 'ta', 'gz', 'gy')
- grad_first: float32 [9, 2, 1, 2, 4, 4], replicated
- grad_second: float32 [9, 1, 2, 2, 4, 4], replicated
Inputs may be any that keep to these rules, and one draw needn't show every extreme that they name: `gauge_links`: every site's four link matrices are unitary 3 x 3 complex matrices of determinant one.
All inputs are finite; a program needn't handle non-finite values.
Results may differ from a plain program's by a relative error of at most 0.0003.
Values sent between devices are 32-bit elements; how exact they have to be, the bound alone decides.
A program may use at most 128 MiB of HBM per device.

v0:
```python
import functools

import jax
import jax.numpy as jnp
import numpy as np
from jax import lax
from jax.experimental import pallas as pl
from jax.experimental.pallas import tpu as pltpu
from jax.sharding import PartitionSpec as P

BLK = 4
NNULL = 24
LT = 4
LZ = 4
LX = 32
LANES = 128
ROWS = LT * LZ
WIDE = LZ * 3 * LANES
STACK = 80
BARE_MASS = -0.5
MESH = pl.DeviceIdType.MESH
F32 = jnp.float32
BF16 = jnp.bfloat16


def dirac_matrix():
    paulis = [
        np.array([[0, 1], [1, 0]], dtype=complex),
        np.array([[0, -1j], [1j, 0]], dtype=complex),
        np.array([[1, 0], [0, -1]], dtype=complex),
    ]
    corners = [-1j * matrix for matrix in paulis] + [np.eye(2, dtype=complex)]
    terms = [(4.0 + BARE_MASS) * np.eye(4)]
    for corner in corners:
        gamma = np.zeros((4, 4), dtype=complex)
        gamma[:2, 2:] = corner
        gamma[2:, :2] = corner.conj().T
        terms.append(-0.5 * (np.eye(4) - gamma))
        terms.append(-0.5 * (np.eye(4) + gamma))
    whole = np.zeros((16, STACK), dtype=np.float32)
    for path, term in enumerate(terms):
        block = np.block([[term.real, -term.imag], [term.imag, term.real]])
        whole[:8, path * 8 : path * 8 + 8] = block
    return np.concatenate([whole, whole], axis=1)


def whole_matrix(weights):
    real_part = weights[:, :, :, 0]
    imag_part = weights[:, :, :, 1]
    blocks = jnp.stack([jnp.stack([real_part, -imag_part]), jnp.stack([imag_part, real_part])])
    arranged = jnp.transpose(blocks, (3, 0, 5, 2, 4, 1, 6))
    return arranged.reshape(weights.shape[1] * 8, weights.shape[0], weights.shape[2] * 8)


def split_left(matrix):
    high = lax.reduce_precision(matrix, 8, 7)
    low = matrix - high
    both = jnp.concatenate([high, low], axis=0)
    return jnp.concatenate([both, both], axis=1).astype(BF16)


def kernel(
    sizes,
    source_ref,
    links_ref,
    null_hbm,
    dirac_ref,
    first_ref,
    second_ref,
    back_ref,
    out_ref,
    coarse_ref,
    grad_ref,
    null_ref,
    et,
    ez,
    dt,
    dz,
    ys,
    yr,
    dy,
    field,
    stack,
    x_first,
    hid,
    mixed,
    total,
    miss,
    cot,
    sums,
    spread_ref,
    red_y,
    red_z,
    red_t,
    send_sem,
    recv_sem,
    red_send,
    red_recv,
    null_sem,
):
    nt, nz, ny = sizes
    it = lax.axis_index("ta")
    iz = lax.axis_index("gz")
    iy = lax.axis_index("gy")
    null_copy = pltpu.make_async_copy(null_hbm, null_ref, null_sem)
    null_copy.start()

    barrier = pltpu.get_barrier_semaphore()
    for axis, mine, count in (("gy", iy, ny), ("gz", iz, nz), ("ta", it, nt)):
        for step in range(1, count):
            pl.semaphore_signal(
                barrier,
                inc=1,
                device_id={axis: lax.rem(mine + step, count)},
                device_id_type=MESH,
            )
    pl.semaphore_wait(barrier, nt + nz + ny - 3)

    row_id = lax.broadcasted_iota(jnp.int32, (8, LANES), 0)
    lane = lax.broadcasted_iota(jnp.int32, (8, LANES), 1)
    column = lane % LX
    sign = jnp.where(row_id < 4, -1.0, 1.0).astype(F32)
    wrap = it == nt - 1

    def link(mu, t, z):
        row = t * LZ + z

        def part(which, a, b):
            base = ((mu * 2 + which) * 9 + a * 3 + b) * ROWS
            return jnp.broadcast_to(links_ref[pl.ds(base + row, 1), :], (8, LANES))

        return part

    def turned(values):
        return [pltpu.roll(v, 4, 0) * sign for v in values]

    def time_sign(mu, t, values):
        if mu != 3:
            return values
        factor = jnp.where(jnp.logical_and(wrap, t == LT - 1), -1.0, 1.0).astype(F32)
        return [v * factor for v in values]

    def forward(mu, t, z, values):
        values = time_sign(mu, t, values)
        part = link(mu, t, z)
        spun = turned(values)
        outs = []
        for a in range(3):
            acc = None
            for b in range(3):
                term = part(0, a, b) * values[b] + part(1, a, b) * spun[b]
                acc = term if acc is None else acc + term
            outs.append(acc)
        return outs

    def adjoint(mu, t, z, values):
        values = time_sign(mu, t, values)
        part = link(mu, t, z)
        spun = turned(values)
        outs = []
        for a in range(3):
            acc = None
            for b in range(3):
                term = part(0, b, a) * values[b] - part(1, b, a) * spun[b]
                acc = term if acc is None else acc + term
            outs.append(acc)
        return outs

    def over_time(body, count=LT):
        def step(t, carry):
            body(t)
            return carry

        lax.fori_loop(0, count, step, 0)

    def exchange(rd, src_up, src_dn, put):
        def send(which, src, dst, axis, target):
            copy = pltpu.make_async_remote_copy(
                src_ref=src,
                dst_ref=dst,
                send_sem=send_sem.at[rd, which],
                recv_sem=recv_sem.at[rd, which],
                device_id={axis: target},
                device_id_type=MESH,
            )
            copy.start()
            return copy

        def y_part(t):
            ups, downs = [], []
            for z in range(LZ):
                up = src_up(1, t, z)
                down = adjoint(1, t, z, src_dn(1, t, z))
                for c in range(3):
                    dy[t, z, c] = down[c]
                ups.append(up)
                downs.append(down)

            def pack(f0, f1, d1, d0):
                left = jnp.where(lane < 32, f0, pltpu.roll(f1, 32, 1))
                right = jnp.where(lane < 96, pltpu.roll(d1, 96, 1), d0)
                return jnp.where(lane < 64, left, right)

            for z in range(LZ):
                ys[rd, t, z] = pack(ups[z][0], ups[z][1], downs[z][1], downs[z][0])
            for h in range(2):
                ys[rd, t, 4 + h] = pack(
                    ups[2 * h][2], ups[2 * h + 1][2], downs[2 * h + 1][2], downs[2 * h][2]
                )

        over_time(y_part)
        other = lax.rem(iy + 1, ny)
        c_y = send(0, ys.at[rd], yr.at[rd], "gy", other)

        def face_part(t):
            for z in range(LZ):
                up_t = src_up(3, t, z)
                up_z = src_up(2, t, z)
                for c in range(3):
                    et[rd, t, z, c] = up_t[c]
                    ez[rd, z, t, c] = up_z[c]

        over_time(face_part)
        c_tu = send(1, et.at[rd, 0], et.at[rd, LT], "ta", lax.rem(it + nt - 1, nt))
        c_zu = send(2, ez.at[rd, 0], ez.at[rd, LZ], "gz", lax.rem(iz + nz - 1, nz))

        def carry_t(t):
            for z in range(LZ):
                down = adjoint(3, t, z, src_dn(3, t, z))
                for c in range(3):
                    dt[rd, t + 1, z, c] = down[c]

        def carry_z(t, zs):
            for z in zs:
                down = adjoint(2, t, z, src_dn(2, t, z))
                for c in range(3):
                    dz[rd, z + 1, t, c] = down[c]

        carry_t(LT - 1)
        c_td = send(3, dt.at[rd, LT], dt.at[rd, 0], "ta", lax.rem(it + 1, nt))
        over_time(lambda t: carry_z(t, (LZ - 1,)))
        c_zd = send(4, dz.at[rd, LZ], dz.at[rd, 0], "gz", lax.rem(iz + 1, nz))

        over_time(carry_t, LT - 1)
        over_time(lambda t: carry_z(t, range(LZ - 1)))

        def x_part(t):
            for z in range(LZ):
                up = [
                    jnp.where(column == LX - 1, pltpu.roll(v, LX - 1, 1), pltpu.roll(v, LANES - 1, 1))
                    for v in src_up(0, t, z)
                ]
                put(1, t, z, forward(0, t, z, up))
                down = [
                    jnp.where(column == 0, pltpu.roll(v, LANES + 1 - LX, 1), pltpu.roll(v, 1, 1))
                    for v in adjoint(0, t, z, src_dn(0, t, z))
                ]
                put(2, t, z, down)

        over_time(x_part)
        c_tu.wait()
        c_td.wait()

        def t_part(t):
            for z in range(LZ):
                put(7, t, z, forward(3, t, z, [et[rd, t + 1, z, c] for c in range(3)]))
                put(8, t, z, [dt[rd, t, z, c] for c in range(3)])

        over_time(t_part)
        c_zu.wait()
        c_zd.wait()

        def z_part(t):
            for z in range(LZ):
                put(5, t, z, forward(2, t, z, [ez[rd, z + 1, t, c] for c in range(3)]))
                put(6, t, z, [dz[rd, z, t, c] for c in range(3)])

        over_time(z_part)
        c_y.wait()

        def y_take(t):
            for z in range(LZ):
                first = yr[rd, t, z]
                third = yr[rd, t, 4 + z // 2]
                f0, d0 = first, first
                f1, d1 = pltpu.roll(first, 96, 1), pltpu.roll(first, 32, 1)
                if z % 2 == 0:
                    f2, d2 = third, third
                else:
                    f2, d2 = pltpu.roll(third, 96, 1), pltpu.roll(third, 32, 1)
                up = src_up(1, t, z)
                up = [
                    pltpu.roll(jnp.where(lane < 32, halo, v), 96, 1)
                    for halo, v in zip((f0, f1, f2), up)
                ]
                put(3, t, z, forward(1, t, z, up))
                down = [
                    pltpu.roll(jnp.where(lane >= 96, halo, dy[t, z, c]), 32, 1)
                    for c, halo in enumerate((d0, d1, d2))
                ]
                put(4, t, z, down)

        over_time(y_take)

    def from_field(mu, t, z):
        return [field[t, z, c] for c in range(3)]

    def put_stack(path, t, z, values):
        for c in range(3):
            stack[t, z, c, path * 8 : path * 8 + 8, :] = values[c]

    def put_swapped(path, t, z, values):
        put_stack(path + 1 if path % 2 == 1 else path - 1, t, z, values)

    def split(values):
        high = values.astype(BF16)
        low = (values - high.astype(F32)).astype(BF16)
        return jnp.concatenate([high, low], axis=0)

    def identity_path():
        def step(t):
            for z in range(LZ):
                for c in range(3):
                    stack[t, z, c, 0:8, :] = field[t, z, c]

        over_time(step)

    def stacked_columns(t):
        return jnp.concatenate(
            [split(stack[t, z, c]) for z in range(LZ) for c in range(3)], axis=1
        )

    def dot(left, right):
        return lax.dot_general(
            left, right, (((1,), (0,)), ((), ())), preferred_element_type=F32
        )

    def dot_t(left, right):
        return lax.dot_general(
            left, right, (((1,), (1,)), ((), ())), preferred_element_type=F32
        )

    def load_source(ref):
        def step(t):
            for z in range(LZ):
                for c in range(3):
                    field[t, z, c] = ref[pl.ds(c * ROWS + t * LZ + z, 8, stride=3 * ROWS), :]

        over_time(step)

    def clear(t):
        for z in range(LZ):
            for c in range(3):
                stack[t, z, c, 72:80, :] = jnp.zeros((8, LANES), F32)

    over_time(clear)

    load_source(source_ref)
    identity_path()
    exchange(0, from_field, from_field, put_stack)

    def residual_step(t):
        result = dot(dirac_ref[...], stacked_columns(t))
        for z in range(LZ):
            for c in range(3):
                j = (z * 3 + c) * LANES
                field[t, z, c] = result[0:8, j : j + LANES]

    over_time(residual_step)

    identity_path()
    exchange(1, from_field, from_field, put_stack)

    def hidden_step(t):
        columns = stacked_columns(t)
        x_first[t] = columns
        result = dot(first_ref[...], columns)
        hid[t] = split(result[0:16] + result[16:32])
        product = dot(second_ref[...], hid[t])
        product = product[0:STACK] + product[STACK : 2 * STACK]
        for z in range(LZ):
            for c in range(3):
                j = (z * 3 + c) * LANES
                mixed[t, z, c] = product[:, j : j + LANES]
                total[t, z, c] = product[0:8, j : j + LANES]

    over_time(hidden_step)

    def mixed_up(mu, t, z):
        k = (1 + 2 * mu) * 8
        return [mixed[t, z, c, k : k + 8, :] for c in range(3)]

    def mixed_dn(mu, t, z):
        k = (2 + 2 * mu) * 8
        return [mixed[t, z, c, k : k + 8, :] for c in range(3)]

    def put_total(path, t, z, values):
        for c in range(3):
            total[t, z, c] += values[c]

    exchange(2, mixed_up, mixed_dn, put_total)

    def store_out(t):
        for z in range(LZ):
            for c in range(3):
                out_ref[pl.ds(c * ROWS + t * LZ + z, 8, stride=3 * ROWS), :] = total[t, z, c]

    over_time(store_out)
    miss[...] = out_ref[...] - source_ref[...]
    null_copy.wait()

    def restrict_step(k, carry):
        re = jnp.zeros((ROWS, LANES), F32)
        im = jnp.zeros((ROWS, LANES), F32)
        for j in range(12):
            v_re = null_ref[pl.ds(pl.multiple_of((k * 24 + j) * ROWS, ROWS), ROWS), :].astype(F32)
            v_im = null_ref[
                pl.ds(pl.multiple_of((k * 24 + 12 + j) * ROWS, ROWS), ROWS), :
            ].astype(F32)
            m_re = miss[j * ROWS : (j + 1) * ROWS, :]
            m_im = miss[(12 + j) * ROWS : (13 + j) * ROWS, :]
            re = re + (v_re * m_re + v_im * m_im)
            im = im + (v_re * m_im - v_im * m_re)
        sums[pl.ds(k, 1), :] = jnp.sum(re, axis=0, keepdims=True)
        sums[pl.ds(NNULL + k, 1), :] = jnp.sum(im, axis=0, keepdims=True)
        return carry

    lax.fori_loop(0, NNULL, restrict_step, 0)
    left = lax.broadcasted_iota(jnp.int32, (LANES, LANES), 0) % LX // BLK
    right = lax.broadcasted_iota(jnp.int32, (LANES, LANES), 1)
    highest = lax.Precision.HIGHEST
    flat = sums[...]
    same = (left == right % LX // BLK).astype(F32)
    pick = (left == right).astype(F32)
    spread_ref[...] = jnp.dot(flat, same, precision=highest, preferred_element_type=F32)
    coarse_ref[...] = jnp.dot(flat, pick, precision=highest, preferred_element_type=F32)

    scale = 2.0 / (ROWS * LANES * nt * nz * ny)

    def prolong_step(j, carry):
        re = miss[pl.ds(pl.multiple_of(j * ROWS, ROWS), ROWS), :]
        im = miss[pl.ds(pl.multiple_of((12 + j) * ROWS, ROWS), ROWS), :]
        for k in range(NNULL):
            v_re = null_ref[pl.ds(pl.multiple_of((k * 24 + j) * ROWS, ROWS), ROWS), :].astype(F32)
            v_im = null_ref[
                pl.ds(pl.multiple_of((k * 24 + 12 + j) * ROWS, ROWS), ROWS), :
            ].astype(F32)
            s_re = spread_ref[k : k + 1, :]
            s_im = spread_ref[NNULL + k : NNULL + k + 1, :]
            re = re + (s_re * v_re - s_im * v_im)
            im = im + (s_re * v_im + s_im * v_re)
        cot[pl.ds(pl.multiple_of(j * ROWS, ROWS), ROWS), :] = re * scale
        cot[pl.ds(pl.multiple_of((12 + j) * ROWS, ROWS), ROWS), :] = im * scale
        return carry

    lax.fori_loop(0, 12, prolong_step, 0)

    load_source(cot)
    identity_path()
    exchange(3, from_field, from_field, put_swapped)

    def back_step(t, carry):
        first_sum, second_sum = carry
        columns = stacked_columns(t)
        result = dot(back_ref[...], columns)
        back = split(result[0:16] + result[16:32])
        first_cols = x_first[t]
        g1 = dot_t(back, first_cols[0:STACK]) + dot_t(back, first_cols[STACK : 2 * STACK])
        g2 = dot_t(hid[t], columns[0:STACK]) + dot_t(hid[t], columns[STACK : 2 * STACK])
        return first_sum + g1[0:16] + g1[16:32], second_sum + g2[0:16] + g2[16:32]

    zero = jnp.zeros((16, STACK), F32)
    first_sum, second_sum = lax.fori_loop(0, LT, back_step, (zero, zero))

    grad_ref[...] = jnp.zeros_like(grad_ref)
    grad_ref[0:16, 0:STACK] = first_sum
    grad_ref[16:32, 0:STACK] = second_sum
    base = 0
    for axis, mine, count, slots in (
        ("gy", iy, ny, red_y),
        ("gz", iz, nz, red_z),
        ("ta", it, nt, red_t),
    ):
        slots[mine] = grad_ref[...]
        copies = []
        for step in range(1, count):
            copy = pltpu.make_async_remote_copy(
                src_ref=slots.at[mine],
                dst_ref=slots.at[mine],
                send_sem=red_send.at[base + step],
                recv_sem=red_recv.at[base + step],
                device_id={axis: lax.rem(mine + step, count)},
                device_id_type=MESH,
            )
            copy.start()
            copies.append(copy)
        for copy in copies:
            copy.wait()
        acc = slots[0]
        for j in range(1, count):
            acc = acc + slots[j]
        grad_ref[...] = acc
        base += count


def body(sizes, source, gauge_links, near_null, w_first, w_second):
    nt, nz, ny = sizes
    first = whole_matrix(w_first).reshape(16, 72)
    second = jnp.transpose(whole_matrix(w_second), (1, 0, 2)).reshape(72, 16)
    first_left = split_left(jnp.pad(first, ((0, 0), (0, 8))))
    second_pad = jnp.pad(second, ((0, 8), (0, 0)))
    second_left = split_left(second_pad)
    back_left = split_left(second_pad.T)
    vmem = pl.BlockSpec(memory_space=pltpu.VMEM)
    slab = (3, 8, LANES)
    out, coarse, grad = pl.pallas_call(
        functools.partial(kernel, sizes),
        out_shape=(
            jax.ShapeDtypeStruct((24 * ROWS, LANES), F32),
            jax.ShapeDtypeStruct((2 * NNULL, LANES), F32),
            jax.ShapeDtypeStruct((32, LANES), F32),
        ),
        in_specs=[vmem, vmem, pl.BlockSpec(memory_space=pl.ANY), vmem, vmem, vmem, vmem],
        out_specs=(vmem, vmem, vmem),
        scratch_shapes=[
            pltpu.VMEM((NNULL * 24 * ROWS, LANES), BF16),
            pltpu.VMEM((4, LT + 1, LZ) + slab, F32),
            pltpu.VMEM((4, LZ + 1, LT) + slab, F32),
            pltpu.VMEM((4, LT + 1, LZ) + slab, F32),
            pltpu.VMEM((4, LZ + 1, LT) + slab, F32),
            pltpu.VMEM((4, LT, 6, 8, LANES), F32),
            pltpu.VMEM((4, LT, 6, 8, LANES), F32),
            pltpu.VMEM((LT, LZ) + slab, F32),
            pltpu.VMEM((LT, LZ) + slab, F32),
            pltpu.VMEM((LT, LZ, 3, STACK, LANES), F32),
            pltpu.VMEM((LT, 2 * STACK, WIDE), BF16),
            pltpu.VMEM((LT, 32, WIDE), BF16),
            pltpu.VMEM((LT, LZ, 3, STACK, LANES), F32),
            pltpu.VMEM((LT, LZ) + slab, F32),
            pltpu.VMEM((24 * ROWS, LANES), F32),
            pltpu.VMEM((24 * ROWS, LANES), F32),
            pltpu.VMEM((2 * NNULL, LANES), F32),
            pltpu.VMEM((2 * NNULL, LANES), F32),
            pltpu.VMEM((ny, 32, LANES), F32),
            pltpu.VMEM((nz, 32, LANES), F32),
            pltpu.VMEM((nt, 32, LANES), F32),
            pltpu.SemaphoreType.DMA((4, 5)),
            pltpu.SemaphoreType.DMA((4, 5)),
            pltpu.SemaphoreType.DMA((nt + nz + ny,)),
            pltpu.SemaphoreType.DMA((nt + nz + ny,)),
            pltpu.SemaphoreType.DMA,
        ],
        compiler_params=pltpu.CompilerParams(
            collective_id=0, has_side_effects=True, vmem_limit_bytes=48 * 1024 * 1024
        ),
    )(
        source.reshape(24 * ROWS, LANES),
        gauge_links.reshape(72 * ROWS, LANES),
        near_null.reshape(NNULL * 24 * ROWS, LANES),
        jnp.asarray(dirac_matrix(), BF16),
        first_left,
        second_left,
        back_left,
    )

    one = grad[0:16, 0:72].reshape(2, 2, 4, 9, 1, 2, 4)
    two = jnp.transpose(grad[16:32, 0:72].reshape(2, 2, 4, 9, 2, 4, 1), (6, 4, 5, 3, 0, 1, 2))

    def merge(product):
        real_grad = product[:, 0, :, :, :, 0] + product[:, 1, :, :, :, 1]
        imag_grad = product[:, 1, :, :, :, 0] - product[:, 0, :, :, :, 1]
        return jnp.transpose(jnp.stack([real_grad, imag_grad]), (3, 1, 4, 0, 2, 5))

    return (
        out.reshape(source.shape),
        coarse[:, : LX // BLK].reshape(2, NNULL, 1, 1, LX // BLK),
        merge(one),
        merge(two),
    )


def solution(mesh):
    sizes = (mesh.shape["ta"], mesh.shape["gz"], mesh.shape["gy"])
    in_specs = (
        P(None, None, None, "ta", "gz", "gy"),
        P(None, None, None, None, "ta", "gz", "gy"),
        P(None, None, None, None, "ta", "gz", "gy"),
        P(),
        P(),
    )
    out_specs = (P(None, None, None, "ta", "gz", "gy"), P(None, None, "ta", "gz", "gy"), P(), P())
    return jax.shard_map(
        functools.partial(body, sizes),
        mesh=mesh,
        in_specs=in_specs,
        out_specs=out_specs,
        check_vma=False,
    )
```

profile of v0, /device:TPU:0, one launch (start us, length us, event | category | flops | bytes accessed | tf_op | source)
XLA Modules:
  0.0 57.0 jit_solution(15608242915689336280)
XLA Ops:
  0.6 0.7 %bitcast_negate_fusion.1 = f32[1,9,2,1,4,4]{1,5,4,2,0,3:T(4,128)S(1)} fusion(f32[9,2,1,2,4,4]{0,5,4,3,2,1:T(4,128)} %param.9), kind=kLoop, calls=%fused_computation.21 | loop fusion | flops 288 | bytes 2304 | tf_op jit(solution)/shard_map/neg | solution.py:50
  1.4 0.7 %bitcast_negate_fusion = f32[1,9,1,2,4,4]{1,5,4,3,0,2:T(4,128)S(1)} fusion(f32[9,1,2,2,4,4]{0,5,4,3,2,1:T(4,128)} %param.10), kind=kLoop, calls=%fused_computation.20 | loop fusion | flops 288 | bytes 2304 | tf_op jit(solution)/shard_map/neg | solution.py:50
  2.1 0.7 %slice_bitcast_fusion.4 = (f32[1,9,2,1,4,4]{1,5,4,2,0,3:T(4,128)S(1)}, f32[1,9,2,1,4,4]{1,5,4,2,3,0:T(4,128)S(1)}, f32[1,9,2,1,4,4]{1,5,4,2,3,0:T(4,128)S(1)}) fusion(f32[9,2,1,2,4,4]{0,5,4,3,2,1:T(4,128)} %param.9), kind=kLoop, calls=%fused_computation.26 | loop fusion | bytes 5760 | tf_op jit(solution)/shard_map/stack;squeeze | solution.py:50
  2.9 0.7 %slice_bitcast_fusion.1 = (f32[1,9,1,2,4,4]{1,5,4,3,0,2:T(4,128)S(1)}, f32[1,9,1,2,4,4]{1,5,4,3,2,0:T(4,128)S(1)}, f32[1,9,1,2,4,4]{1,5,4,3,2,0:T(4,128)S(1)}) fusion(f32[9,1,2,2,4,4]{0,5,4,3,2,1:T(4,128)} %param.10), kind=kLoop, calls=%fused_computation.23 | loop fusion | bytes 5760 | tf_op jit(solution)/shard_map/stack;squeeze | solution.py:50
  3.7 0.1 copy.87
  3.8 0.1 copy.88
  3.9 0.1 maximum_convert_fusion.1
  4.0 0.1 copy.89.second_ref
  4.1 0.3 copy.82
  4.5 0.2 reshape_reshape.3
  4.6 0.1 pad_maximum_fusion
  4.7 0.0 copy-start
  4.7 1.7 %copy-done = bf16[24,2,4,3,4,4,128]{6,5,4,3,2,1,0:T(4,128)(2,1)S(1)} copy-done((bf16[24,2,4,3,4,4,128]{6,5,4,3,2,1,0:T(4,128)(2,1)S(1)}, bf16[24,2,4,3,4,4,128]{6,5,4,3,2,1,0:T(4,128)(2,1)}, u32[]{:S(2)}) %copy-start) | copy-done | bytes 2359320
  6.4 0.0 copy-start.1
  6.4 1.1 %copy-done.1 = f32[4,2,3,3,4,4,128]{6,5,4,3,2,1,0:T(4,128)S(1)} copy-done((f32[4,2,3,3,4,4,128]{6,5,4,3,2,1,0:T(4,128)S(1)}, f32[4,2,3,3,4,4,128]{6,5,4,3,2,1,0:T(4,128)}, u32[]{:S(2)}) %copy-start.1) | copy-done | bytes 589848
  7.5 0.0 copy-start.2
  7.5 0.9 %copy-done.2 = f32[2,4,3,4,4,128]{5,4,3,2,1,0:T(4,128)S(1)} copy-done((f32[2,4,3,4,4,128]{5,4,3,2,1,0:T(4,128)S(1)}, f32[2,4,3,4,4,128]{5,4,3,2,1,0:T(4,128)}, u32[]{:S(2)}) %copy-start.2) | copy-done | bytes 196632
  8.4 0.0 copy-start.3
  8.4 0.7 %copy-done.3 = bf16[16,160]{1,0:T(8,128)(2,1)S(1)} copy-done((bf16[16,160]{1,0:T(8,128)(2,1)S(1)}, bf16[16,160]{1,0:T(8,128)(2,1)}, u32[]{:S(2)}) %copy-start.3) | copy-done | bytes 5144
  9.1 44.3 %shard_map.93 = (f32[384,128]{1,0:T(8,128)S(1)}, f32[48,128]{1,0:T(8,128)S(1)}, f32[32,128]{1,0:T(8,128)S(1)}) custom-call(f32[384,128]{1,0:T(8,128)S(1)} %bitcast.68, f32[1152,128]{1,0:T(8,128)S(1)} %bitcast.67, bf16[9216,128]{1,0:T(8,128)(2,1)S(1)} %bitcast.66, bf16[16,160]{1,0:T(8,128)(2,1)S(1)} %copy-done.3, ...), custom_call_target="tpu_custom_call" | custom-call | tf_op jit(solution)/shard_map/pallas_call | solution.py:516
  53.4 0.7 %copy.94 = f32[2,24,1,1,8]{1,4,3,2,0:T(8,128)} copy(f32[2,24,1,1,8]{4,1,0,3,2:T(8,128)S(1)} %bitcast.70) | data formatting | bytes 3072
  54.0 0.2 reshape.161
  54.2 0.1 slice_add_fusion
  54.3 0.1 copy.92
  54.4 0.1 copy.93
  54.6 0.6 %copy.96 = f32[9,1,2,2,4,4]{0,5,4,3,2,1:T(4,128)} copy(f32[9,1,2,2,4,4]{0,5,2,4,1,3:T(4,128)S(1)} %maximum_bitcast_fusion.7) | data formatting | bytes 4608
  55.2 0.2 reshape.160
  55.3 0.1 fusion.1
  55.4 0.1 copy.90
  55.6 0.1 copy.91
  55.7 0.6 %copy.95 = f32[9,2,1,2,4,4]{0,5,4,3,2,1:T(4,128)} copy(f32[9,2,1,2,4,4]{0,5,2,4,1,3:T(4,128)S(1)} %maximum_bitcast_fusion.6) | data formatting | bytes 4608
  56.3 0.7 %copy.100 = f32[2,4,3,4,4,128]{5,4,3,2,1,0:T(4,128)} copy(f32[2,4,3,4,4,128]{5,4,3,2,1,0:T(4,128)S(1)} %bitcast.69) | data formatting | bytes 393216
  (16 shorter events, 0.2 us)
Async XLA Ops:
  4.7 1.7 %copy-start = (bf16[24,2,4,3,4,4,128]{6,5,4,3,2,1,0:T(4,128)(2,1)S(1)}, bf16[24,2,4,3,4,4,128]{6,5,4,3,2,1,0:T(4,128)(2,1)}, u32[]{:S(2)}) copy-start(bf16[24,2,4,3,4,4,128]{6,5,4,3,2,1,0:T(4,128)(2,1)} %param.8) | copy-start | bytes 7077892
  6.4 1.1 %copy-start.1 = (f32[4,2,3,3,4,4,128]{6,5,4,3,2,1,0:T(4,128)S(1)}, f32[4,2,3,3,4,4,128]{6,5,4,3,2,1,0:T(4,128)}, u32[]{:S(2)}) copy-start(f32[4,2,3,3,4,4,128]{6,5,4,3,2,1,0:T(4,128)} %param.7) | copy-start | bytes 1769476
  7.5 0.9 %copy-start.2 = (f32[2,4,3,4,4,128]{5,4,3,2,1,0:T(4,128)S(1)}, f32[2,4,3,4,4,128]{5,4,3,2,1,0:T(4,128)}, u32[]{:S(2)}) copy-start(f32[2,4,3,4,4,128]{5,4,3,2,1,0:T(4,128)} %param.6) | copy-start | bytes 589828
  8.4 0.7 %copy-start.3 = (bf16[16,160]{1,0:T(8,128)(2,1)S(1)}, bf16[16,160]{1,0:T(8,128)(2,1)}, u32[]{:S(2)}) copy-start(bf16[16,160]{1,0:T(8,128)(2,1)} %constant.5.clone.dirac_ref) | copy-start | bytes 15364
where the time goes:
time: 57.5 us; the launch traced here: 57 us
  Pallas kernels  44.3 us (77%)
  local copies, waits for them, and re-layouts  10 us (17%)
  other arithmetic  1.94 us (3%)
  between operations  0.77 us (1%)
    pallas_call x1, Pallas kernels, body(): pl.pallas_call(functools.partial(kernel, sizes), out_shape=(jax.ShapeDtyp...  44.3 us
    unnamed x12, local copies, waits for them, and re-layouts  6.93 us
    another operation x2, local copies, waits for them, and re-layouts, whole_matrix(): jnp.stack([real_part, -imag_part])  1.49 us
    neg x2, other arithmetic, whole_matrix(): -imag_part  1.45 us

commit v1 on v0

--- a/solution.py
+++ b/solution.py
@@ -44,34 +44,74 @@
     return np.concatenate([whole, whole], axis=1)
 
 
-def whole_matrix(weights):
-    real_part = weights[:, :, :, 0]
-    imag_part = weights[:, :, :, 1]
-    blocks = jnp.stack([jnp.stack([real_part, -imag_part]), jnp.stack([imag_part, real_part])])
-    arranged = jnp.transpose(blocks, (3, 0, 5, 2, 4, 1, 6))
-    return arranged.reshape(weights.shape[1] * 8, weights.shape[0], weights.shape[2] * 8)
-
-
-def split_left(matrix):
-    high = lax.reduce_precision(matrix, 8, 7)
-    low = matrix - high
-    both = jnp.concatenate([high, low], axis=0)
-    return jnp.concatenate([both, both], axis=1).astype(BF16)
+def index_maps(width):
+    row = lax.broadcasted_iota(jnp.int32, (128, width), 0)
+    col = lax.broadcasted_iota(jnp.int32, (128, width), 1)
+    mask = jnp.where(row < 64, row % 4, row // 4 % 4) == col % 4
+    return mask, col // 4 % 2
+
+
+def left_maps(shape, row_dim, mat_dim):
+    row = lax.broadcasted_iota(jnp.int32, shape, row_dim)
+    mat = lax.broadcasted_iota(jnp.int32, shape, mat_dim)
+    first = row < 64
+    part, part_mat = row // 16 % 2, mat // 4 % 2
+    match = jnp.logical_and(row // 32 == mat // 8, jnp.where(first, row // 4 % 4, row % 4) == mat % 4)
+    same = part == part_mat
+    sign_same = jnp.where(jnp.logical_or(first, part_mat == 0), 1.0, -1.0)
+    sign_cross = jnp.where(jnp.logical_and(first, part_mat == 0), -1.0, 1.0)
+    keep = jnp.where(jnp.logical_and(match, same), sign_same, 0.0).astype(F32)
+    swap = jnp.where(jnp.logical_and(match, jnp.logical_not(same)), sign_cross, 0.0).astype(F32)
+    return keep, swap
+
+
+def exact_dot(left, right):
+    return jnp.dot(left, right, precision=lax.Precision.HIGHEST, preferred_element_type=F32)
+
+
+def spread_weights(values):
+    width = 2 * STACK
+    row = lax.broadcasted_iota(jnp.int32, (9, width), 0)
+    col = lax.broadcasted_iota(jnp.int32, (9, width), 1)
+    path = (row == jnp.where(col >= STACK, col - STACK, col) // 8).astype(F32)
+    wide = exact_dot(values, path)
+    mask, kind = index_maps(width)
+    keep, swap = left_maps((32, 128), 1, 0)
+    wide = jnp.where(mask, wide, 0.0)
+    straight = jnp.where(kind == 0, wide, 0.0)
+    return exact_dot(keep, straight) + exact_dot(swap, wide - straight)
+
+
+def gather_weights(product):
+    keep, swap = left_maps((128, 32), 0, 1)
+    mask, kind = index_maps(STACK)
+    wide = jnp.where(kind == 0, exact_dot(keep, product), exact_dot(swap, product))
+    wide = jnp.where(mask, wide, 0.0)
+    row = lax.broadcasted_iota(jnp.int32, (STACK, 9), 0)
+    col = lax.broadcasted_iota(jnp.int32, (STACK, 9), 1)
+    return exact_dot(wide, (row // 8 == col).astype(F32))
 
 
 def kernel(
     sizes,
+    source_hbm,
+    links_hbm,
+    null_hbm,
+    w_first_hbm,
+    w_second_hbm,
+    dirac_hbm,
+    out_ref,
+    coarse_ref,
+    weight_ref,
     source_ref,
     links_ref,
-    null_hbm,
+    null_ref,
+    w_ref,
     dirac_ref,
     first_ref,
     second_ref,
     back_ref,
-    out_ref,
-    coarse_ref,
     grad_ref,
-    null_ref,
     et,
     ez,
     dt,
@@ -96,14 +136,34 @@
     recv_sem,
     red_send,
     red_recv,
-    null_sem,
+    load_sem,
 ):
     nt, nz, ny = sizes
     it = lax.axis_index("ta")
     iz = lax.axis_index("gz")
     iy = lax.axis_index("gy")
-    null_copy = pltpu.make_async_copy(null_hbm, null_ref, null_sem)
-    null_copy.start()
+    link_rows = 18 * ROWS
+
+    def link_slice(ref, mu):
+        return ref.at[pl.ds(mu * link_rows, link_rows), :]
+
+    loads = [
+        (source_hbm, source_ref),
+        (link_slice(links_hbm, 1), link_slice(links_ref, 1)),
+        (link_slice(links_hbm, 3), link_slice(links_ref, 3)),
+        (link_slice(links_hbm, 2), link_slice(links_ref, 2)),
+        (link_slice(links_hbm, 0), link_slice(links_ref, 0)),
+        (dirac_hbm, dirac_ref),
+        (w_first_hbm, w_ref.at[0]),
+        (w_second_hbm, w_ref.at[1]),
+        (null_hbm, null_ref),
+    ]
+    loads = [
+        pltpu.make_async_copy(src, dst, load_sem.at[k]) for k, (src, dst) in enumerate(loads)
+    ]
+    for load in loads:
+        load.start()
+    null_copy = loads.pop()
 
     barrier = pltpu.get_barrier_semaphore()
     for axis, mine, count in (("gy", iy, ny), ("gz", iz, nz), ("ta", it, nt)):
@@ -173,7 +233,7 @@
 
         lax.fori_loop(0, count, step, 0)
 
-    def exchange(rd, src_up, src_dn, put):
+    def exchange(rd, src_up, src_dn, put, meanwhile=None):
         def send(which, src, dst, axis, target):
             copy = pltpu.make_async_remote_copy(
                 src_ref=src,
@@ -258,6 +318,8 @@
                 put(2, t, z, down)
 
         over_time(x_part)
+        if meanwhile is not None:
+            meanwhile()
         c_tu.wait()
         c_td.wait()
 
@@ -355,12 +417,29 @@
 
     over_time(clear)
 
+    def prepare():
+        for load in loads[5:]:
+            load.wait()
+        values = spread_weights(w_ref[...].reshape(128, 9))
+        high = values.astype(BF16)
+        low = values - high.astype(F32)
+        low = low.astype(BF16)
+        first_ref[...] = jnp.concatenate([high[0:16], low[0:16]], axis=0)
+        back_ref[...] = jnp.concatenate([high[16:32], low[16:32]], axis=0)
+        col = lax.broadcasted_iota(jnp.int32, (16, 2 * STACK), 1)
+        mixing = jnp.where(col < STACK, high[16:32].astype(F32), low[16:32].astype(F32))
+        mixing = jnp.concatenate([mixing, mixing], axis=0)
+        second_ref[...] = jnp.transpose(mixing).astype(BF16)
+
+    loads[0].wait()
     load_source(source_ref)
     identity_path()
-    exchange(0, from_field, from_field, put_stack)
+    for load in loads[1:5]:
+        load.wait()
+    exchange(0, from_field, from_field, put_stack, prepare)
 
     def residual_step(t):
-        result = dot(dirac_ref[...], stacked_columns(t))
+        result = dot(dirac_ref[...].astype(BF16), stacked_columns(t))
         for z in range(LZ):
             for c in range(3):
                 j = (z * 3 + c) * LANES
@@ -427,13 +506,18 @@
 
     lax.fori_loop(0, NNULL, restrict_step, 0)
     left = lax.broadcasted_iota(jnp.int32, (LANES, LANES), 0) % LX // BLK
-    right = lax.broadcasted_iota(jnp.int32, (LANES, LANES), 1)
-    highest = lax.Precision.HIGHEST
-    flat = sums[...]
-    same = (left == right % LX // BLK).astype(F32)
-    pick = (left == right).astype(F32)
-    spread_ref[...] = jnp.dot(flat, same, precision=highest, preferred_element_type=F32)
-    coarse_ref[...] = jnp.dot(flat, pick, precision=highest, preferred_element_type=F32)
+    right = lax.broadcasted_iota(jnp.int32, (LANES, LANES), 1) % LX // BLK
+    spread_ref[...] = exact_dot(sums[...], (left == right).astype(F32))
+    block = lax.broadcasted_iota(jnp.int32, (8, LANES), 0)
+    pick = (block == column // BLK).astype(F32)
+    for half in range(2):
+        coarse_ref[half * 8 : half * 8 + 8, :] = lax.dot_general(
+            pick,
+            sums[half * NNULL : (half + 1) * NNULL, :],
+            (((1,), (1,)), ((), ())),
+            precision=lax.Precision.HIGHEST,
+            preferred_element_type=F32,
+        )
 
     scale = 2.0 / (ROWS * LANES * nt * nz * ny)
 
@@ -501,29 +585,47 @@
             acc = acc + slots[j]
         grad_ref[...] = acc
         base += count
+    weight_ref[...] = gather_weights(grad_ref[:, 0:STACK])
+
+
+def store_kernel(out_ref, coarse_ref, weight_ref, out_hbm, coarse_hbm, first_hbm, second_hbm, sem):
+    pairs = [
+        (out_ref, out_hbm),
+        (coarse_ref, coarse_hbm),
+        (weight_ref.at[0:64, :], first_hbm),
+        (weight_ref.at[64:128, :], second_hbm),
+    ]
+    copies = [pltpu.make_async_copy(src, dst, sem.at[k]) for k, (src, dst) in enumerate(pairs)]
+    for copy in copies:
+        copy.start()
+    for copy in copies:
+        copy.wait()
 
 
 def body(sizes, source, gauge_links, near_null, w_first, w_second):
     nt, nz, ny = sizes
-    first = whole_matrix(w_first).reshape(16, 72)
-    second = jnp.transpose(whole_matrix(w_second), (1, 0, 2)).reshape(72, 16)
-    first_left = split_left(jnp.pad(first, ((0, 0), (0, 8))))
-    second_pad = jnp.pad(second, ((0, 8), (0, 0)))
-    second_left = split_left(second_pad)
-    back_left = split_left(second_pad.T)
     vmem = pl.BlockSpec(memory_space=pltpu.VMEM)
     slab = (3, 8, LANES)
+    hbm = pl.BlockSpec(memory_space=pltpu.HBM)
     out, coarse, grad = pl.pallas_call(
         functools.partial(kernel, sizes),
         out_shape=(
             jax.ShapeDtypeStruct((24 * ROWS, LANES), F32),
-            jax.ShapeDtypeStruct((2 * NNULL, LANES), F32),
-            jax.ShapeDtypeStruct((32, LANES), F32),
+            jax.ShapeDtypeStruct((16, NNULL), F32),
+            jax.ShapeDtypeStruct((128, 9), F32),
         ),
-        in_specs=[vmem, vmem, pl.BlockSpec(memory_space=pl.ANY), vmem, vmem, vmem, vmem],
+        in_specs=[hbm] * 6,
         out_specs=(vmem, vmem, vmem),
         scratch_shapes=[
+            pltpu.VMEM((24 * ROWS, LANES), F32),
+            pltpu.VMEM((72 * ROWS, LANES), F32),
             pltpu.VMEM((NNULL * 24 * ROWS, LANES), BF16),
+            pltpu.VMEM((2, 64, 9), F32),
+            pltpu.VMEM((16, 2 * STACK), F32),
+            pltpu.VMEM((32, 2 * STACK), BF16),
+            pltpu.VMEM((2 * STACK, 32), BF16),
+            pltpu.VMEM((32, 2 * STACK), BF16),
+            pltpu.VMEM((32, LANES), F32),
             pltpu.VMEM((4, LT + 1, LZ) + slab, F32),
             pltpu.VMEM((4, LZ + 1, LT) + slab, F32),
             pltpu.VMEM((4, LT + 1, LZ) + slab, F32),
@@ -548,34 +650,40 @@
             pltpu.SemaphoreType.DMA((4, 5)),
             pltpu.SemaphoreType.DMA((nt + nz + ny,)),
             pltpu.SemaphoreType.DMA((nt + nz + ny,)),
-            pltpu.SemaphoreType.DMA,
+            pltpu.SemaphoreType.DMA((9,)),
         ],
         compiler_params=pltpu.CompilerParams(
-            collective_id=0, has_side_effects=True, vmem_limit_bytes=48 * 1024 * 1024
+            collective_id=0, has_side_effects=True, vmem_limit_bytes=(65536 - 288) * 1024
         ),
     )(
         source.reshape(24 * ROWS, LANES),
         gauge_links.reshape(72 * ROWS, LANES),
         near_null.reshape(NNULL * 24 * ROWS, LANES),
-        jnp.asarray(dirac_matrix(), BF16),
-        first_left,
-        second_left,
-        back_left,
+        jnp.transpose(w_first, (1, 2, 3, 4, 5, 0)).reshape(64, 9),
+        jnp.transpose(w_second, (1, 2, 3, 4, 5, 0)).reshape(64, 9),
+        jnp.asarray(dirac_matrix()),
     )
-
-    one = grad[0:16, 0:72].reshape(2, 2, 4, 9, 1, 2, 4)
-    two = jnp.transpose(grad[16:32, 0:72].reshape(2, 2, 4, 9, 2, 4, 1), (6, 4, 5, 3, 0, 1, 2))
-
-    def merge(product):
-        real_grad = product[:, 0, :, :, :, 0] + product[:, 1, :, :, :, 1]
-        imag_grad = product[:, 1, :, :, :, 0] - product[:, 0, :, :, :, 1]
-        return jnp.transpose(jnp.stack([real_grad, imag_grad]), (3, 1, 4, 0, 2, 5))
+    out, coarse, first, second = pl.pallas_call(
+        store_kernel,
+        out_shape=(
+            jax.ShapeDtypeStruct((24 * ROWS, LANES), F32),
+            jax.ShapeDtypeStruct((16, NNULL), F32),
+            jax.ShapeDtypeStruct((64, 9), F32),
+            jax.ShapeDtypeStruct((64, 9), F32),
+        ),
+        in_specs=[vmem] * 3,
+        out_specs=(hbm,) * 4,
+        scratch_shapes=[pltpu.SemaphoreType.DMA((4,))],
+    )(out, coarse, grad)
+
+    def as_weights(values, outs, ins):
+        return jnp.transpose(values.reshape(outs, ins, 2, 4, 4, 9), (5, 0, 1, 2, 3, 4))
 
     return (
         out.reshape(source.shape),
-        coarse[:, : LX // BLK].reshape(2, NNULL, 1, 1, LX // BLK),
-        merge(one),
-        merge(two),
+        jnp.transpose(coarse.reshape(2, 1, 1, LX // BLK, NNULL), (0, 4, 1, 2, 3)),
+        as_weights(first, 2, 1),
+        as_weights(second, 1, 2),
     )
 
 

time: 57.5 us -> 48.1 us (0.84)
  local copies, waits for them, and re-layouts: 10 us -> 0 us
  Pallas kernels: 44.3 us -> 47.3 us
  other arithmetic: 1.94 us -> 0 us
    unnamed x12 -> x0, local copies, waits for them, and re-layouts: 6.93 us -> none
    pallas_call x0 -> x1, Pallas kernels: none -> 1.68 us  [body(): pl.pallas_call(store_kernel, out_shape=(jax.ShapeDtypeStruct((24 * ROWS,...]
    another operation x3 -> x0, local copies, waits for them, and re-layouts: 1.64 us -> none  [the longest x2 1.49 us: whole_matrix(): jnp.stack([real_part, -imag_part])]
    neg x2 -> x0, other arithmetic: 1.45 us -> none  [whole_matrix(): -imag_part]
    pallas_call x1, Pallas kernels: 44.3 us -> 45.6 us  [body(): pl.pallas_call(functools.partial(kernel, sizes), out_shape=(jax.ShapeDtyp...]
where the time goes in v1:
time: 48.1 us; the launch traced here: 47.9 us
  Pallas kernels  47.3 us (98%)
  between operations  0.64 us (1%)
    pallas_call x1, Pallas kernels, body(): pl.pallas_call(functools.partial(kernel, sizes), out_shape=(jax.ShapeDtyp...  45.6 us
    pallas_call x1, Pallas kernels, body(): pl.pallas_call(store_kernel, out_shape=(jax.ShapeDtypeStruct((24 * ROWS,...  1.68 us

profile of v1, /device:TPU:0, one launch (start us, length us, event | category | flops | bytes accessed | tf_op | source)
XLA Modules:
  0.0 47.9 jit_solution(2636189255061465559)
XLA Ops:
  0.6 45.6 %shard_map.93 = (f32[384,128]{1,0:T(8,128)}, f32[16,24]{1,0:T(8,128)}, f32[128,9]{1,0:T(8,128)}) custom-call(f32[384,128]{1,0:T(8,128)} %bitcast.25, f32[1152,128]{1,0:T(8,128)} %bitcast.24, bf16[9216,128]{1,0:T(8,128)(2,1)} %bitcast.23, f32[64,9]{1,0:T(8,128)} %bitcast.26, f32[64,9]{1,0:T(8,128)} %bitcast.27, f32[16,160]{1,0:T(8,128)} %constant.2.clone.dirac_hbm), custom_call_target="tpu_custom_call" | custom-call | tf_op jit(solution)/shard_map/pallas_call | solution.py:610
  46.3 1.7 %shard_map.94 = (f32[384,128]{1,0:T(8,128)}, f32[16,24]{1,0:T(8,128)}, f32[64,9]{1,0:T(8,128)}, f32[64,9]{1,0:T(8,128)}) custom-call(f32[384,128]{1,0:T(8,128)} %get-tuple-element.11.out_ref, f32[16,24]{1,0:T(8,128)} %get-tuple-element.12.coarse_ref, f32[128,9]{1,0:T(8,128)} %get-tuple-element.13.weight_ref), custom_call_target="tpu_custom_call" | custom-call | tf_op jit(solution)/shard_map/pallas_call | solution.py:666

commit v2 on v1

--- a/solution.py
+++ b/solution.py
@@ -112,12 +112,8 @@
     second_ref,
     back_ref,
     grad_ref,
-    et,
-    ez,
-    dt,
-    dz,
-    ys,
-    yr,
+    out_face,
+    in_face,
     dy,
     field,
     stack,
@@ -130,7 +126,6 @@
     sums,
     spread_ref,
     red_y,
-    red_z,
     red_t,
     send_sem,
     recv_sem,
@@ -166,15 +161,15 @@
     null_copy = loads.pop()
 
     barrier = pltpu.get_barrier_semaphore()
-    for axis, mine, count in (("gy", iy, ny), ("gz", iz, nz), ("ta", it, nt)):
-        for step in range(1, count):
-            pl.semaphore_signal(
-                barrier,
-                inc=1,
-                device_id={axis: lax.rem(mine + step, count)},
-                device_id_type=MESH,
-            )
-    pl.semaphore_wait(barrier, nt + nz + ny - 3)
+    plane = [
+        {"gz": lax.rem(iz + a, nz), "gy": lax.rem(iy + b, ny)}
+        for a in range(nz)
+        for b in range(ny)
+    ][1:]
+    column_of = [{"ta": lax.rem(it + a, nt)} for a in range(1, nt)]
+    for partner in plane + column_of:
+        pl.semaphore_signal(barrier, inc=1, device_id=partner, device_id_type=MESH)
+    pl.semaphore_wait(barrier, len(plane) + len(column_of))
 
     row_id = lax.broadcasted_iota(jnp.int32, (8, LANES), 0)
     lane = lax.broadcasted_iota(jnp.int32, (8, LANES), 1)
@@ -184,25 +179,26 @@
 
     def link(mu, t, z):
         row = t * LZ + z
+        held = {}
 
         def part(which, a, b):
-            base = ((mu * 2 + which) * 9 + a * 3 + b) * ROWS
-            return jnp.broadcast_to(links_ref[pl.ds(base + row, 1), :], (8, LANES))
+            if (which, a, b) not in held:
+                base = ((mu * 2 + which) * 9 + a * 3 + b) * ROWS
+                held[which, a, b] = jnp.broadcast_to(
+                    links_ref[pl.ds(base + row, 1), :], (8, LANES)
+                )
+            return held[which, a, b]
 
         return part
 
     def turned(values):
         return [pltpu.roll(v, 4, 0) * sign for v in values]
 
-    def time_sign(mu, t, values):
-        if mu != 3:
-            return values
-        factor = jnp.where(jnp.logical_and(wrap, t == LT - 1), -1.0, 1.0).astype(F32)
+    def time_edge(values):
+        factor = jnp.where(wrap, -1.0, 1.0).astype(F32)
         return [v * factor for v in values]
 
-    def forward(mu, t, z, values):
-        values = time_sign(mu, t, values)
-        part = link(mu, t, z)
+    def forward(part, values):
         spun = turned(values)
         outs = []
         for a in range(3):
@@ -213,9 +209,7 @@
             outs.append(acc)
         return outs
 
-    def adjoint(mu, t, z, values):
-        values = time_sign(mu, t, values)
-        part = link(mu, t, z)
+    def adjoint(part, values):
         spun = turned(values)
         outs = []
         for a in range(3):
@@ -233,11 +227,11 @@
 
         lax.fori_loop(0, count, step, 0)
 
-    def exchange(rd, src_up, src_dn, put, meanwhile=None):
-        def send(which, src, dst, axis, target):
+    def exchange(rd, src_up, src_dn, put, meanwhile=None, ready=None):
+        def send(which, axis, target):
             copy = pltpu.make_async_remote_copy(
-                src_ref=src,
-                dst_ref=dst,
+                src_ref=out_face.at[rd, which],
+                dst_ref=in_face.at[rd, which],
                 send_sem=send_sem.at[rd, which],
                 recv_sem=recv_sem.at[rd, which],
                 device_id={axis: target},
@@ -246,123 +240,143 @@
             copy.start()
             return copy
 
-        def y_part(t):
-            ups, downs = [], []
+        def quarters(values, shift):
+            a, b, c, d = [
+                pltpu.roll(v, (32 * k + shift) % LANES, 1) if (32 * k + shift) % LANES else v
+                for k, v in enumerate(values)
+            ]
+            return jnp.where(
+                lane < 64, jnp.where(lane < 32, a, b), jnp.where(lane < 96, c, d)
+            )
+
+        def unpacked(which, t, c, z, shift):
+            value = in_face[rd, which, t, c]
+            amount = (-32 * z - shift) % LANES
+            return pltpu.roll(value, amount, 1) if amount else value
+
+        def y_up(t):
+            ups = [src_up(1, t, z) for z in range(LZ)]
+            for c in range(3):
+                out_face[rd, 0, t, c] = quarters([up[c] for up in ups], 0)
+
+        def y_down(t):
+            downs = [adjoint(link(1, t, z), src_dn(1, t, z)) for z in range(LZ)]
+            for c in range(3):
+                for z in range(LZ):
+                    dy[t, z, c] = downs[z][c]
+                out_face[rd, 3, t, c] = quarters([down[c] for down in downs], 32)
+
+        other = lax.rem(iy + 1, ny)
+        t_before, t_after = lax.rem(it + nt - 1, nt), lax.rem(it + 1, nt)
+        z_before, z_after = lax.rem(iz + nz - 1, nz), lax.rem(iz + 1, nz)
+        over_time(y_up)
+        c_yu = send(0, "gy", other)
+        for z in range(LZ):
+            values = src_up(3, 0, z)
+            for c in range(3):
+                out_face[rd, 1, z, c] = values[c]
+        c_tu = send(1, "ta", t_before)
+        for t in range(LT):
+            values = src_up(2, t, 0)
+            for c in range(3):
+                out_face[rd, 2, t, c] = values[c]
+        c_zu = send(2, "gz", z_before)
+        if ready is not None:
+            ready(1)
+        over_time(y_down)
+        c_yd = send(3, "gy", other)
+        if ready is not None:
+            ready(3)
+        for z in range(LZ):
+            values = adjoint(link(3, LT - 1, z), time_edge(src_dn(3, LT - 1, z)))
+            for c in range(3):
+                out_face[rd, 4, z, c] = values[c]
+        c_td = send(4, "ta", t_after)
+        if ready is not None:
+            ready(2)
+
+        def z_down(t):
+            values = adjoint(link(2, t, LZ - 1), src_dn(2, t, LZ - 1))
+            for c in range(3):
+                out_face[rd, 5, t, c] = values[c]
+
+        over_time(z_down)
+        c_zd = send(5, "gz", z_after)
+
+        def t_inner(t):
             for z in range(LZ):
-                up = src_up(1, t, z)
-                down = adjoint(1, t, z, src_dn(1, t, z))
-                for c in range(3):
-                    dy[t, z, c] = down[c]
-                ups.append(up)
-                downs.append(down)
-
-            def pack(f0, f1, d1, d0):
-                left = jnp.where(lane < 32, f0, pltpu.roll(f1, 32, 1))
-                right = jnp.where(lane < 96, pltpu.roll(d1, 96, 1), d0)
-                return jnp.where(lane < 64, left, right)
-
-            for z in range(LZ):
-                ys[rd, t, z] = pack(ups[z][0], ups[z][1], downs[z][1], downs[z][0])
-            for h in range(2):
-                ys[rd, t, 4 + h] = pack(
-                    ups[2 * h][2], ups[2 * h + 1][2], downs[2 * h + 1][2], downs[2 * h][2]
-                )
-
-        over_time(y_part)
-        other = lax.rem(iy + 1, ny)
-        c_y = send(0, ys.at[rd], yr.at[rd], "gy", other)
-
-        def face_part(t):
-            for z in range(LZ):
-                up_t = src_up(3, t, z)
-                up_z = src_up(2, t, z)
-                for c in range(3):
-                    et[rd, t, z, c] = up_t[c]
-                    ez[rd, z, t, c] = up_z[c]
-
-        over_time(face_part)
-        c_tu = send(1, et.at[rd, 0], et.at[rd, LT], "ta", lax.rem(it + nt - 1, nt))
-        c_zu = send(2, ez.at[rd, 0], ez.at[rd, LZ], "gz", lax.rem(iz + nz - 1, nz))
-
-        def carry_t(t):
-            for z in range(LZ):
-                down = adjoint(3, t, z, src_dn(3, t, z))
-                for c in range(3):
-                    dt[rd, t + 1, z, c] = down[c]
-
-        def carry_z(t, zs):
-            for z in zs:
-                down = adjoint(2, t, z, src_dn(2, t, z))
-                for c in range(3):
-                    dz[rd, z + 1, t, c] = down[c]
-
-        carry_t(LT - 1)
-        c_td = send(3, dt.at[rd, LT], dt.at[rd, 0], "ta", lax.rem(it + 1, nt))
-        over_time(lambda t: carry_z(t, (LZ - 1,)))
-        c_zd = send(4, dz.at[rd, LZ], dz.at[rd, 0], "gz", lax.rem(iz + 1, nz))
-
-        over_time(carry_t, LT - 1)
-        over_time(lambda t: carry_z(t, range(LZ - 1)))
+                part = link(3, t, z)
+                put(7, t, z, forward(part, src_up(3, t + 1, z)))
+                put(8, t + 1, z, adjoint(part, src_dn(3, t, z)))
+
+        over_time(t_inner, LT - 1)
+
+        def z_inner(t):
+            for z in range(LZ - 1):
+                part = link(2, t, z)
+                put(5, t, z, forward(part, src_up(2, t, z + 1)))
+                put(6, t, z + 1, adjoint(part, src_dn(2, t, z)))
+
+        over_time(z_inner)
+        if ready is not None:
+            ready(0)
 
         def x_part(t):
             for z in range(LZ):
+                part = link(0, t, z)
                 up = [
                     jnp.where(column == LX - 1, pltpu.roll(v, LX - 1, 1), pltpu.roll(v, LANES - 1, 1))
                     for v in src_up(0, t, z)
                 ]
-                put(1, t, z, forward(0, t, z, up))
+                put(1, t, z, forward(part, up))
                 down = [
                     jnp.where(column == 0, pltpu.roll(v, LANES + 1 - LX, 1), pltpu.roll(v, 1, 1))
-                    for v in adjoint(0, t, z, src_dn(0, t, z))
+                    for v in adjoint(part, src_dn(0, t, z))
                 ]
                 put(2, t, z, down)
 
         over_time(x_part)
         if meanwhile is not None:
             meanwhile()
+        c_yu.wait()
+
+        def y_up_take(t):
+            for z in range(LZ):
+                up = [
+                    pltpu.roll(jnp.where(lane < 32, unpacked(0, t, c, z, 0), v), 96, 1)
+                    for c, v in enumerate(src_up(1, t, z))
+                ]
+                put(3, t, z, forward(link(1, t, z), up))
+
+        over_time(y_up_take)
         c_tu.wait()
-        c_td.wait()
-
-        def t_part(t):
+        for z in range(LZ):
+            up = time_edge([in_face[rd, 1, z, c] for c in range(3)])
+            put(7, LT - 1, z, forward(link(3, LT - 1, z), up))
+        c_zu.wait()
+
+        def z_up_take(t):
+            up = [in_face[rd, 2, t, c] for c in range(3)]
+            put(5, t, LZ - 1, forward(link(2, t, LZ - 1), up))
+
+        over_time(z_up_take)
+        c_yd.wait()
+
+        def y_down_take(t):
             for z in range(LZ):
-                put(7, t, z, forward(3, t, z, [et[rd, t + 1, z, c] for c in range(3)]))
-                put(8, t, z, [dt[rd, t, z, c] for c in range(3)])
-
-        over_time(t_part)
-        c_zu.wait()
-        c_zd.wait()
-
-        def z_part(t):
-            for z in range(LZ):
-                put(5, t, z, forward(2, t, z, [ez[rd, z + 1, t, c] for c in range(3)]))
-                put(6, t, z, [dz[rd, z, t, c] for c in range(3)])
-
-        over_time(z_part)
-        c_y.wait()
-
-        def y_take(t):
-            for z in range(LZ):
-                first = yr[rd, t, z]
-                third = yr[rd, t, 4 + z // 2]
-                f0, d0 = first, first
-                f1, d1 = pltpu.roll(first, 96, 1), pltpu.roll(first, 32, 1)
-                if z % 2 == 0:
-                    f2, d2 = third, third
-                else:
-                    f2, d2 = pltpu.roll(third, 96, 1), pltpu.roll(third, 32, 1)
-                up = src_up(1, t, z)
-                up = [
-                    pltpu.roll(jnp.where(lane < 32, halo, v), 96, 1)
-                    for halo, v in zip((f0, f1, f2), up)
-                ]
-                put(3, t, z, forward(1, t, z, up))
                 down = [
-                    pltpu.roll(jnp.where(lane >= 96, halo, dy[t, z, c]), 32, 1)
-                    for c, halo in enumerate((d0, d1, d2))
+                    pltpu.roll(jnp.where(lane >= 96, unpacked(3, t, c, z, 32), dy[t, z, c]), 32, 1)
+                    for c in range(3)
                 ]
                 put(4, t, z, down)
 
-        over_time(y_take)
+        over_time(y_down_take)
+        c_td.wait()
+        for z in range(LZ):
+            put(8, 0, z, [in_face[rd, 4, z, c] for c in range(3)])
+        c_zd.wait()
+        for t in range(LT):
+            put(6, t, 0, [in_face[rd, 5, t, c] for c in range(3)])
 
     def from_field(mu, t, z):
         return [field[t, z, c] for c in range(3)]
@@ -434,9 +448,11 @@
     loads[0].wait()
     load_source(source_ref)
     identity_path()
-    for load in loads[1:5]:
-        load.wait()
-    exchange(0, from_field, from_field, put_stack, prepare)
+
+    def ready(mu):
+        loads[(4, 1, 3, 2)[mu]].wait()
+
+    exchange(0, from_field, from_field, put_stack, prepare, ready)
 
     def residual_step(t):
         result = dot(dirac_ref[...].astype(BF16), stacked_columns(t))
@@ -560,20 +576,16 @@
     grad_ref[0:16, 0:STACK] = first_sum
     grad_ref[16:32, 0:STACK] = second_sum
     base = 0
-    for axis, mine, count, slots in (
-        ("gy", iy, ny, red_y),
-        ("gz", iz, nz, red_z),
-        ("ta", it, nt, red_t),
-    ):
+    for partners, mine, slots in ((plane, iz * ny + iy, red_y), (column_of, it, red_t)):
         slots[mine] = grad_ref[...]
         copies = []
-        for step in range(1, count):
+        for step, partner in enumerate(partners):
             copy = pltpu.make_async_remote_copy(
                 src_ref=slots.at[mine],
                 dst_ref=slots.at[mine],
                 send_sem=red_send.at[base + step],
                 recv_sem=red_recv.at[base + step],
-                device_id={axis: lax.rem(mine + step, count)},
+                device_id=partner,
                 device_id_type=MESH,
             )
             copy.start()
@@ -581,10 +593,10 @@
         for copy in copies:
             copy.wait()
         acc = slots[0]
-        for j in range(1, count):
+        for j in range(1, len(partners) + 1):
             acc = acc + slots[j]
         grad_ref[...] = acc
-        base += count
+        base += len(partners)
     weight_ref[...] = gather_weights(grad_ref[:, 0:STACK])
 
 
@@ -626,12 +638,8 @@
             pltpu.VMEM((2 * STACK, 32), BF16),
             pltpu.VMEM((32, 2 * STACK), BF16),
             pltpu.VMEM((32, LANES), F32),
-            pltpu.VMEM((4, LT + 1, LZ) + slab, F32),
-            pltpu.VMEM((4, LZ + 1, LT) + slab, F32),
-            pltpu.VMEM((4, LT + 1, LZ) + slab, F32),
-            pltpu.VMEM((4, LZ + 1, LT) + slab, F32),
-            pltpu.VMEM((4, LT, 6, 8, LANES), F32),
-            pltpu.VMEM((4, LT, 6, 8, LANES), F32),
+            pltpu.VMEM((4, 6, 4) + slab, F32),
+            pltpu.VMEM((4, 6, 4) + slab, F32),
             pltpu.VMEM((LT, LZ) + slab, F32),
             pltpu.VMEM((LT, LZ) + slab, F32),
             pltpu.VMEM((LT, LZ, 3, STACK, LANES), F32),
@@ -643,13 +651,12 @@
             pltpu.VMEM((24 * ROWS, LANES), F32),
             pltpu.VMEM((2 * NNULL, LANES), F32),
             pltpu.VMEM((2 * NNULL, LANES), F32),
-            pltpu.VMEM((ny, 32, LANES), F32),
-            pltpu.VMEM((nz, 32, LANES), F32),
+            pltpu.VMEM((ny * nz, 32, LANES), F32),
             pltpu.VMEM((nt, 32, LANES), F32),
-            pltpu.SemaphoreType.DMA((4, 5)),
-            pltpu.SemaphoreType.DMA((4, 5)),
-            pltpu.SemaphoreType.DMA((nt + nz + ny,)),
-            pltpu.SemaphoreType.DMA((nt + nz + ny,)),
+            pltpu.SemaphoreType.DMA((4, 6)),
+            pltpu.SemaphoreType.DMA((4, 6)),
+            pltpu.SemaphoreType.DMA((nt + nz * ny,)),
+            pltpu.SemaphoreType.DMA((nt + nz * ny,)),
             pltpu.SemaphoreType.DMA((9,)),
         ],
         compiler_params=pltpu.CompilerParams(

time: 48.1 us -> 44.1 us (0.917)
  Pallas kernels: 47.3 us -> 43.3 us
    pallas_call x1, Pallas kernels: 45.6 us -> 41.6 us  [body(): pl.pallas_call(functools.partial(kernel, sizes), out_shape=(jax.ShapeDtyp...]
where the time goes in v2:
time: 44.1 us; the launch traced here: 43.9 us
  Pallas kernels  43.3 us (98%)
  between operations  0.64 us (1%)
    pallas_call x1, Pallas kernels, body(): pl.pallas_call(functools.partial(kernel, sizes), out_shape=(jax.ShapeDtyp...  41.6 us
    pallas_call x1, Pallas kernels, body(): pl.pallas_call(store_kernel, out_shape=(jax.ShapeDtypeStruct((24 * ROWS,...  1.68 us

profile of v2, /device:TPU:0, one launch (start us, length us, event | category | flops | bytes accessed | tf_op | source)
XLA Modules:
  0.0 43.9 jit_solution(13890063763721255855)
XLA Ops:
  0.6 41.6 %shard_map.93 = (f32[384,128]{1,0:T(8,128)}, f32[16,24]{1,0:T(8,128)}, f32[128,9]{1,0:T(8,128)}) custom-call(f32[384,128]{1,0:T(8,128)} %bitcast.25, f32[1152,128]{1,0:T(8,128)} %bitcast.24, bf16[9216,128]{1,0:T(8,128)(2,1)} %bitcast.23, f32[64,9]{1,0:T(8,128)} %bitcast.26, f32[64,9]{1,0:T(8,128)} %bitcast.27, f32[16,160]{1,0:T(8,128)} %constant.2.clone.dirac_hbm), custom_call_target="tpu_custom_call" | custom-call | tf_op jit(solution)/shard_map/pallas_call | solution.py:622
  42.3 1.7 %shard_map.94 = (f32[384,128]{1,0:T(8,128)}, f32[16,24]{1,0:T(8,128)}, f32[64,9]{1,0:T(8,128)}, f32[64,9]{1,0:T(8,128)}) custom-call(f32[384,128]{1,0:T(8,128)} %get-tuple-element.11.out_ref, f32[16,24]{1,0:T(8,128)} %get-tuple-element.12.coarse_ref, f32[128,9]{1,0:T(8,128)} %get-tuple-element.13.weight_ref), custom_call_target="tpu_custom_call" | custom-call | tf_op jit(solution)/shard_map/pallas_call | solution.py:673

commit v3 on v2

--- a/solution.py
+++ b/solution.py
@@ -225,7 +225,7 @@
             body(t)
             return carry
 
-        lax.fori_loop(0, count, step, 0)
+        lax.fori_loop(0, count, step, 0, unroll=True)
 
     def exchange(rd, src_up, src_dn, put, meanwhile=None, ready=None):
         def send(which, axis, target):
@@ -570,7 +570,7 @@
         return first_sum + g1[0:16] + g1[16:32], second_sum + g2[0:16] + g2[16:32]
 
     zero = jnp.zeros((16, STACK), F32)
-    first_sum, second_sum = lax.fori_loop(0, LT, back_step, (zero, zero))
+    first_sum, second_sum = lax.fori_loop(0, LT, back_step, (zero, zero), unroll=True)
 
     grad_ref[...] = jnp.zeros_like(grad_ref)
     grad_ref[0:16, 0:STACK] = first_sum

time: 44.1 us -> 40.6 us (0.921)
  Pallas kernels: 43.3 us -> 39.8 us
    pallas_call x1, Pallas kernels: 41.6 us -> 38.1 us  [body(): pl.pallas_call(functools.partial(kernel, sizes), out_shape=(jax.ShapeDtyp...]
where the time goes in v3:
time: 40.6 us; the launch traced here: 40.4 us
  Pallas kernels  39.8 us (98%)
  between operations  0.64 us (2%)
    pallas_call x1, Pallas kernels, body(): pl.pallas_call(functools.partial(kernel, sizes), out_shape=(jax.ShapeDtyp...  38.1 us
    pallas_call x1, Pallas kernels, body(): pl.pallas_call(store_kernel, out_shape=(jax.ShapeDtypeStruct((24 * ROWS,...  1.68 us

profile of v3, /device:TPU:0, one launch (start us, length us, event | category | flops | bytes accessed | tf_op | source)
XLA Modules:
  0.0 40.4 jit_solution(2489199812977427781)
XLA Ops:
  0.6 38.1 %shard_map.93 = (f32[384,128]{1,0:T(8,128)}, f32[16,24]{1,0:T(8,128)}, f32[128,9]{1,0:T(8,128)}) custom-call(f32[384,128]{1,0:T(8,128)} %bitcast.25, f32[1152,128]{1,0:T(8,128)} %bitcast.24, bf16[9216,128]{1,0:T(8,128)(2,1)} %bitcast.23, f32[64,9]{1,0:T(8,128)} %bitcast.26, f32[64,9]{1,0:T(8,128)} %bitcast.27, f32[16,160]{1,0:T(8,128)} %constant.2.clone.dirac_hbm), custom_call_target="tpu_custom_call" | custom-call | tf_op jit(solution)/shard_map/pallas_call | solution.py:622
  38.8 1.7 %shard_map.94 = (f32[384,128]{1,0:T(8,128)}, f32[16,24]{1,0:T(8,128)}, f32[64,9]{1,0:T(8,128)}, f32[64,9]{1,0:T(8,128)}) custom-call(f32[384,128]{1,0:T(8,128)} %get-tuple-element.11.out_ref, f32[16,24]{1,0:T(8,128)} %get-tuple-element.12.coarse_ref, f32[128,9]{1,0:T(8,128)} %get-tuple-element.13.weight_ref), custom_call_target="tpu_custom_call" | custom-call | tf_op jit(solution)/shard_map/pallas_call | solution.py:673
